TPU v7x, 512 devices: a whole 4x8x8 slice. The times are simulated.
512 devices in a mesh: grp: 4 (over x_hi, core), dev: 128 (over z, x_lo, y).
Axes of the slice: x: 4 (x_hi: 2, x_lo: 2; x = x_hi * 2 + x_lo), y: 8, z: 8, core: 2. Of those that a mesh axis runs over, the one named last changes fastest.
Arguments:
- velocity: float32 [1024, 3, 65536], P('dev', None, 'grp'), parts along dimension 2, may hold values from -6 to 6
- starts: int32 [3], replicated, may hold values from 0 to 512, as said below
- picks: int32 [16384], replicated, may hold values from 0 to 16383, each once
Outputs:
- spectra: float32 [9, 256, 65536], P(None, None, ('grp', 'dev')), parts along dimension 2
- plane_mean: float32 [12, 256], P('grp'), parts along dimension 0
There are 4 independent parts, one for each index of `grp`. A program takes and returns all parts, laid end to end along the dimension named above; an argument that names none is the same for every part. Nothing has to cross between parts.
Inputs may be any that keep to these rules, and one draw needn't show every extreme that they name: The first window starts at 0, the last at 512; window w starts within 64 of w * 256. `picks`: every point appears exactly once.
All inputs are finite; a program needn't handle non-finite values.
Results may differ from a plain program's by a relative error of at most 0.0001.
Values sent between devices are 32-bit elements; how exact they have to be, the bound alone decides.
No kernel may reach another device: no remote copies, remote signals or barrier semaphores. Data moves between devices by JAX's collectives and lax.ppermute only.
A program may use at most 192 MiB of HBM per device.

v0:
```python
import math

import jax
import jax.numpy as jnp
from jax import lax
from jax.sharding import PartitionSpec as P

L = 512
F = 256


def make_tables(length, bins):
    sample = jnp.arange(length, dtype=jnp.int32)
    freq = jnp.arange(bins, dtype=jnp.int32)
    phase = (freq[:, None] * sample[None, :] % length).astype(jnp.float32) * (
        2.0 * math.pi / length
    )
    basis = jnp.concatenate([jnp.cos(phase), -jnp.sin(phase)], axis=0)
    taper = 0.5 - 0.5 * jnp.cos(sample.astype(jnp.float32) * (2.0 * math.pi / length))
    return (basis, taper)


def series_spectra(series, starts, basis, taper, length, bins):
    count = starts.shape[0]
    width = series.shape[2]
    scale = 1.0 / (jnp.sum(taper * taper) * count)
    pairs = ((0, 1), (0, 2), (1, 2))

    def window_step(totals, begin):
        frame = lax.dynamic_slice_in_dim(series, begin, length, 0)
        centred = frame - jnp.mean(frame, axis=0, keepdims=True)
        tapered = (centred * taper[:, None, None]).reshape(length, 3 * width)
        result = jnp.dot(
            basis, tapered, precision=lax.Precision.HIGHEST, preferred_element_type=jnp.float32
        )
        result = result.reshape(2, bins, 3, width)
        real_part, imag_part = (result[0], result[1])
        rows = []
        for comp in range(3):
            rows.append(real_part[:, comp] ** 2 + imag_part[:, comp] ** 2)
        for first, second in pairs:
            rows.append(
                real_part[:, first] * real_part[:, second]
                + imag_part[:, first] * imag_part[:, second]
            )
        for first, second in pairs:
            rows.append(
                real_part[:, first] * imag_part[:, second]
                - imag_part[:, first] * real_part[:, second]
            )
        return (totals + jnp.stack(rows, axis=0), None)

    empty = jnp.zeros((9, bins, width), jnp.float32)
    totals, unused = lax.scan(window_step, empty, starts)
    return totals * scale


def on_device(velocity, starts, picks):
    owners = lax.axis_size("dev")
    basis, taper = make_tables(L, F)
    local_times = velocity.shape[0]
    points = velocity.shape[2]
    by_point = jnp.transpose(velocity, (2, 0, 1))
    chosen = jnp.take(by_point, picks, axis=0)
    chosen = chosen.reshape(owners, points // owners, local_times, 3)
    arrived = lax.all_to_all(chosen, "dev", split_axis=0, concat_axis=2, tiled=True)
    series = jnp.transpose(arrived[0], (1, 2, 0))
    spectra = series_spectra(series, starts, basis, taper, L, F)
    own_sum = jnp.sum(spectra[:3], axis=2)
    total = lax.psum(own_sum, "dev")
    plane_mean = total / (spectra.shape[2] * owners)
    return (spectra, plane_mean)


def solution(mesh):
    placed = (P("dev", None, "grp"), P(), P())
    return jax.shard_map(
        on_device,
        mesh=mesh,
        in_specs=placed,
        out_specs=(P(None, None, ("grp", "dev")), P("grp", None)),
        check_vma=False,
    )
```

profile of v0, /device:TPU:4, one launch (start us, length us, event | category | flops | bytes accessed | tf_op | source)
XLA Modules:
  0.0 699.1 jit_solution(12571118354940866278)
XLA Ops:
  0.6 0.9 fusion.9
  1.5 0.9 and_bitcast_fusion
  2.4 21.9 %copy.14 = f32[8,3,16384]{0,1,2:T(4,128)} copy(f32[8,3,16384]{2,0,1:T(8,128)} %param.5) | data formatting | bytes 3145728 | tf_op args[0]
  24.2 260.6 %gather_fusion = f32[16384,8,3]{1,2,0:T(4,128)} fusion(f32[16384,8,3]{1,2,0:T(4,128)} %bitcast.90, s32[16384]{0:T(1024)S(1)} %fusion.9), kind=kCustom, calls=%fused_computation | custom fusion | bytes 3211264 | tf_op jit(solution)/shard_map/jit(_take)/gather | solution.py:64
  284.8 22.5 %copy.15 = f32[128,128,8,3]{1,2,3,0:T(8,128)S(1)} copy(f32[128,128,8,3]{2,3,1,0:T(4,128)} %bitcast.89) | data formatting | bytes 3145728 | tf_op jit(solution)/shard_map/jit(_take)/gather | solution.py:64
  307.3 1.4 broadcast_select_fusion
  308.7 18.4 %all-to-all-start = ((f32[128,128,8,3]{1,2,3,0:T(8,128)}), f32[128,128,8,3]{1,2,3,0:T(8,128)S(1)}, u32[]{:S(2)}, u32[]{:S(2)}) async-start(f32[128,128,8,3]{1,2,3,0:T(8,128)} %broadcast_select_fusion), calls=%async_computation | async-start | bytes 3145728 | tf_op jit(solution)/shard_map/all_to_all | solution.py:66
  327.2 0.6 multiply_reduce_fusion
  328.5 2.1 sine_negate_fusion
  330.6 1.0 pad_maximum_fusion
  331.6 37.5 %all-to-all-done = f32[128,128,8,3]{1,2,3,0:T(8,128)S(1)} async-done(((f32[128,128,8,3]{1,2,3,0:T(8,128)}), f32[128,128,8,3]{1,2,3,0:T(8,128)S(1)}, u32[]{:S(2)}, u32[]{:S(2)}) %all-to-all-start) | async-done | bytes 1572896 | tf_op jit(solution)/shard_map/all_to_all | solution.py:66
  369.1 1.3 copy.22
  370.4 22.3 %while.11 = (s32[]{:T(128)}, f32[9,256,128]{1,2,0:T(8,128)S(1)}, s32[3]{0:T(128)S(1)}, f32[1024,3,128]{2,0,1:T(8,128)}, f32[512,512]{1,0:T(8,128)}, /*index=5*/s32[]{:T(128)}, s32[]{:T(128)}, s32[]{:T(128)}) while((s32[]{:T(128)}, f32[9,256,128]{1,2,0:T(8,128)S(1)}, s32[3]{0:T(128)S(1)}, f32[1024,3,128]{2,0,1:T(8,128)}, ...), condition=%wide.region_2.3_spmd.clone, body=%wide.region_0.2_spmd.clone.sunk | while | flops 1210025984 | bytes 21768364 | solution.py:54
  370.4 0.6 dynamic_slice.12
  372.8 1.2 fusion.20
  374.0 0.3 copy.24
  374.5 1.0 copy-done
  375.5 1.4 convolution_bitcast_fusion.2
  377.4 0.4 select_add_fusion.2
  377.8 0.6 dynamic_slice.12
  380.2 1.2 fusion.20
  382.0 1.0 copy-done
  383.0 1.4 convolution_bitcast_fusion.2
  384.8 0.4 select_add_fusion.2
  385.3 0.6 dynamic_slice.12
  387.7 1.2 fusion.20
  389.4 1.0 copy-done
  390.4 1.4 convolution_bitcast_fusion.2
  392.3 0.4 select_add_fusion.2
  392.7 0.4 copy.18
  393.4 305.2 %psum.7 = f32[3,256]{1,0:T(4,128)S(1)} all-reduce(f32[3,256]{1,0:T(4,128)S(1)} %slice_reduce_fusion), channel_id=1, replica_groups=mesh['grp'=4,'dev'=128] {'dev'}, use_global_device_ids=true, to_apply=%region_5.6 | all-reduce | flops 768 | bytes 6144 | tf_op jit(solution)/shard_map/psum | solution.py:70
  698.5 0.6 broadcast_multiply_fusion.2
  (51 shorter events, 2.3 us)
Async XLA Ops:
  308.7 60.4 %all-to-all-start = ((f32[128,128,8,3]{1,2,3,0:T(8,128)}), f32[128,128,8,3]{1,2,3,0:T(8,128)S(1)}, u32[]{:S(2)}, u32[]{:S(2)}) async-start(f32[128,128,8,3]{1,2,3,0:T(8,128)} %broadcast_select_fusion), calls=%async_computation | async-start | bytes 3145728 | tf_op jit(solution)/shard_map/all_to_all | solution.py:66
  331.6 38.7 %copy-start.2 = (s32[3]{0:T(128)S(1)}, s32[3]{0:T(128)}, u32[]{:S(2)}) copy-start(s32[3]{0:T(128)} %param.6) | copy-start | bytes 40
  374.3 1.2 copy-start
  381.8 1.2 copy-start
  389.2 1.2 copy-start
  393.2 306.0 %copy-start.1 = (f32[9,256,128]{2,1,0:T(8,128)}, f32[9,256,128]{2,1,0:T(8,128)S(1)}, u32[]{:S(2)}) copy-start(f32[9,256,128]{2,1,0:T(8,128)S(1)} %broadcast_multiply_fusion.1) | copy-start | bytes 3538948
where the time goes:
time: 706 us; the launch traced here: 699 us
  local copies, waits for them, and re-layouts  312 us (44%)
  blocking collectives  305 us (43%)
  waiting for transfers between devices  37.5 us (5%)
  starting transfers between devices  18.4 us (3%)
  other arithmetic  14 us (2%)
    psum x1, blocking collectives, on_device(): total = lax.psum(own_sum, 'dev')  305 us
    gather x2, local copies, waits for them, and re-layouts, on_device(): chosen = jnp.take(by_point, picks, axis=0)  283 us
    all_to_all x1, waiting for transfers between devices, on_device(): lax.all_to_all(chosen, 'dev', split_axis=0, concat_axis=2, tiled=True)  37.5 us
    unnamed x5, local copies, waits for them, and re-layouts  21.9 us
    all_to_all x1, starting transfers between devices, on_device(): lax.all_to_all(chosen, 'dev', split_axis=0, concat_axis=2, tiled=True)  18.4 us
  transfers between devices with their start and end apart: 1, of which 1 were waited for; matrix products, arithmetic and copies ran while one was open for 1% of the time, Pallas kernels for 0%

commit v1 on v0

v1 whole, which is shorter than its diff:
```python
import functools

import jax
import jax.numpy as jnp
import ml_dtypes
import numpy as np
from jax import lax
from jax.experimental import pallas as pl
from jax.experimental.pallas import tpu as pltpu
from jax.sharding import Mesh, PartitionSpec as P

L = 512
F = 256
W = 3
LANES = 128
QUARTERS = 4
DEV = ("z", "xl", "y")


def split_bf16(table):
    high = table.astype(ml_dtypes.bfloat16)
    low = (table - high.astype(np.float64)).astype(ml_dtypes.bfloat16)
    return high, low


def make_tables():
    half = np.arange(L // 2)
    bins = np.arange(F // 2)
    bases = []
    for odd in (0, 1):
        phase = ((2 * bins[:, None] + odd) * half[None, :] % L) * (2.0 * np.pi / L)
        bases.append(np.concatenate([np.cos(phase), -np.sin(phase)], axis=0))
    high, low = split_bf16(np.stack(bases))
    turn = np.arange(L) * (2.0 * np.pi / L)
    turns = np.stack([np.cos(turn), np.sin(turn)]).astype(np.float32)
    turns = np.broadcast_to(turns[:, :, None], (2, L, LANES))
    taper = 0.5 - 0.5 * np.cos(turn)
    return high, low, np.ascontiguousarray(turns), float(1.0 / (np.sum(taper * taper) * W))


BASIS_HIGH, BASIS_LOW, TURNS, SCALE = make_tables()


def gather_kernel(
    picks_ref, x_ref, out_ref, picks, x, table, index, even, odd, out, sems, index_sems, x_sems, out_sems
):
    rows, points = x.shape
    blocks = out.shape[0]
    quarter = points // QUARTERS
    apart = LANES // QUARTERS
    pieces = x_sems.shape[0]
    width = quarter // pieces
    chunks = out_sems.shape[0]
    size = blocks // chunks
    together = even.shape[0]

    picks_copy = pltpu.make_async_copy(picks_ref, picks, sems.at[0])
    picks_copy.start()
    x_copies = []
    for piece in range(pieces):
        for q in range(QUARTERS):
            span = pl.ds(q * quarter + piece * width, width)
            x_copies.append(
                pltpu.make_async_copy(x_ref.at[:, span], x.at[:, span], x_sems.at[piece, q])
            )
    for copy in x_copies:
        copy.start()
    picks_copy.wait()
    index[...] = picks[...] % quarter

    def index_copy(slot, first):
        held = (even, odd)[slot]
        return pltpu.make_async_copy(index.at[pl.ds(first, together)], held, index_sems.at[slot])

    index_copy(0, 0).start()
    index_copy(1, together).start()

    pad = jnp.zeros((apart - rows, LANES), jnp.float32)
    for piece in range(pieces):
        for copy in x_copies[piece * QUARTERS : (piece + 1) * QUARTERS]:
            copy.wait()

        for block in range(width // LANES):
            start = piece * width + block * LANES
            parts = []
            for q in range(QUARTERS):
                parts += [x[:, q * quarter + start : q * quarter + start + LANES], pad]
            table[start : start + LANES, :] = jnp.concatenate(parts, axis=0).T

    point_rows = table.reshape(quarter, 1, LANES)
    row = lax.broadcasted_iota(jnp.int32, (8, LANES), 0)

    def pick(held, block):
        tiles = []
        for tile in range(LANES // 8):
            parts = [
                jnp.broadcast_to(point_rows[held[block, tile * 8 + j]], (8, LANES))
                for j in range(8)
            ]
            step = 1
            while len(parts) > 1:
                mask = (row & step) == 0
                parts = [jnp.where(mask, parts[i], parts[i + 1]) for i in range(0, len(parts), 2)]
                step *= 2
            tiles.append(parts[0])
        return jnp.concatenate(tiles, axis=0)

    def keep(block, turned):
        which = jnp.broadcast_to(picks[pl.ds(block, 1), :], (rows, LANES))
        value = turned[0:rows]
        for q in range(1, QUARTERS):
            part = turned[q * apart : q * apart + rows]
            value = jnp.where(which >= q * quarter, part, value)
        out[block] = value

    def batch(held, first, before):
        for i in range(together):
            picked = pick(held, i)
            keep(jnp.maximum(first + i - 1, 0), before.T)
            before = picked
        return before

    def chunk_copy(chunk):
        span = pl.ds(chunk * size, size)
        return pltpu.make_async_copy(out.at[span], out_ref.at[span], out_sems.at[chunk])

    def chunk_step(chunk, before):
        for slot, held in enumerate((even, odd)):
            first = chunk * size + slot * together
            index_copy(slot, first).wait()
            before = batch(held, first, before)

            @pl.when(chunk < chunks - 1)
            def _():
                index_copy(slot, first + size).start()

            if slot == 0:

                @pl.when(chunk > 0)
                def _():
                    chunk_copy(chunk - 1).start()

        return before

    last = lax.fori_loop(0, chunks, chunk_step, jnp.zeros((LANES, LANES), jnp.float32))
    keep(blocks - 1, last.T)
    chunk_copy(chunks - 1).start()

    def finish(chunk, carry):
        chunk_copy(chunk).wait()
        return carry

    lax.fori_loop(0, chunks, finish, 0)


def gather_points(picks, x):
    rows, points = x.shape
    blocks = points // LANES
    pieces = points // QUARTERS // 1024
    vmem = pltpu.VMEM
    return pl.pallas_call(
        gather_kernel,
        out_shape=jax.ShapeDtypeStruct((blocks, rows, LANES), jnp.float32),
        in_specs=[pl.BlockSpec(memory_space=pl.ANY)] * 2,
        out_specs=pl.BlockSpec(memory_space=pl.ANY),
        scratch_shapes=[
            vmem((blocks, LANES), jnp.int32),
            vmem((rows, points), jnp.float32),
            vmem((points // QUARTERS, LANES), jnp.float32),
            vmem((blocks, LANES), jnp.int32),
            pltpu.SMEM((8, LANES), jnp.int32),
            pltpu.SMEM((8, LANES), jnp.int32),
            vmem((blocks, rows, LANES), jnp.float32),
            pltpu.SemaphoreType.DMA((1,)),
            pltpu.SemaphoreType.DMA((2,)),
            pltpu.SemaphoreType.DMA((pieces, QUARTERS)),
            pltpu.SemaphoreType.DMA((8,)),
        ],
        compiler_params=pltpu.CompilerParams(vmem_limit_bytes=58 * 2**20),
        name="gather_points",
    )(picks.reshape(blocks, LANES), x)


def transforms_kernel(points, starts_ref, x_ref, high_ref, low_ref, turns_ref, res_ref, own_ref, power_ref):
    half = L // 2
    sample = lax.broadcasted_iota(jnp.int32, (L, LANES), 0)
    for w in range(W):
        start = starts_ref[w]
        turn = lax.rem(start, L)
        cos_start = turns_ref[0, pl.ds(turn, 1), :]
        sin_start = turns_ref[1, pl.ds(turn, 1), :]
        taper = 0.5 - 0.5 * (turns_ref[0] * cos_start + turns_ref[1] * sin_start)
        late = sample >= start
        terms = [[], []]
        for comp in range(3):
            series = x_ref[:, comp * 8 : comp * 8 + 8, :].reshape(2 * L, LANES)
            frame = jnp.where(late, series[0:L], series[L : 2 * L])
            centred = frame - jnp.sum(frame, axis=0, keepdims=True) * (1.0 / L)
            tapered = centred * taper
            terms[0].append(tapered[0:half] + tapered[half:L])
            terms[1].append(tapered[0:half] - tapered[half:L])
        for odd in (0, 1):
            term = jnp.concatenate(terms[odd], axis=1)
            high = term.astype(jnp.bfloat16)
            low = (term - high.astype(jnp.float32)).astype(jnp.bfloat16)
            dot = functools.partial(jnp.dot, preferred_element_type=jnp.float32)
            res_ref[w, odd] = (
                dot(high_ref[odd], high) + dot(high_ref[odd], low) + dot(low_ref[odd], high)
            )

    for odd in (0, 1):
        power = jnp.zeros((F // 2, 3 * LANES), jnp.float32)
        for w in range(W):
            real, imag = res_ref[w, odd, 0 : F // 2, :], res_ref[w, odd, F // 2 : F, :]
            power += real * real + imag * imag
        for comp in range(3):
            span = slice(comp * LANES, (comp + 1) * LANES)
            power_ref[comp, pl.ds(odd, F // 2, stride=2), :] = power[:, span]
    ones = jnp.ones((8, LANES), jnp.float32)
    for comp in range(3):
        sums = lax.dot_general(
            ones,
            power_ref[comp],
            (((1,), (1,)), ((), ())),
            precision=lax.Precision.HIGHEST,
            preferred_element_type=jnp.float32,
        )
        own_ref[comp : comp + 1, :] = sums[0:1] * (SCALE / points)


def rows_kernel(res_ref, spectra_ref, out_ref, out_sems):
    rows = 8
    bins = F // 2

    def combine(step, carry):
        first = pl.multiple_of(step * rows, rows)
        for odd in (0, 1):
            totals = [None] * 9
            for w in range(W):
                real = [
                    res_ref[w, odd, pl.ds(first, rows), comp * LANES : (comp + 1) * LANES]
                    for comp in range(3)
                ]
                imag = [
                    res_ref[w, odd, pl.ds(bins + first, rows), comp * LANES : (comp + 1) * LANES]
                    for comp in range(3)
                ]
                terms = [real[c] * real[c] + imag[c] * imag[c] for c in range(3)]
                pairs = ((0, 1), (0, 2), (1, 2))
                terms += [real[i] * real[j] + imag[i] * imag[j] for i, j in pairs]
                terms += [real[i] * imag[j] - imag[i] * real[j] for i, j in pairs]
                totals = [b if a is None else a + b for a, b in zip(totals, terms)]
            for row in range(9):
                out_ref[row, pl.ds(2 * first + odd, rows, stride=2), :] = totals[row] * SCALE
        return carry

    pieces = out_sems.shape[0]
    copies = []
    for piece in range(pieces):
        steps = bins // rows // pieces
        lax.fori_loop(piece * steps, (piece + 1) * steps, combine, 0)
        span = pl.ds(piece * (F // pieces), F // pieces)
        copies.append(
            pltpu.make_async_copy(out_ref.at[:, span], spectra_ref.at[:, span], out_sems.at[piece])
        )
        copies[piece].start()
    for copy in copies:
        copy.wait()


def window_transforms(starts, arrived, points):
    vmem = pl.BlockSpec(memory_space=pltpu.VMEM)
    return pl.pallas_call(
        functools.partial(transforms_kernel, points),
        out_shape=(
            jax.ShapeDtypeStruct((W, 2, F, 3 * LANES), jnp.float32),
            jax.ShapeDtypeStruct((3, F), jnp.float32),
        ),
        in_specs=[pl.BlockSpec(memory_space=pltpu.SMEM)] + [vmem] * 4,
        out_specs=(vmem, vmem),
        scratch_shapes=[pltpu.VMEM((3, F, LANES), jnp.float32)],
        compiler_params=pltpu.CompilerParams(vmem_limit_bytes=28 * 2**20),
        name="window_transforms",
    )(starts, arrived, jnp.asarray(BASIS_HIGH), jnp.asarray(BASIS_LOW), jnp.asarray(TURNS))


def spectra_rows(transforms):
    return pl.pallas_call(
        rows_kernel,
        out_shape=jax.ShapeDtypeStruct((9, F, LANES), jnp.float32),
        in_specs=[pl.BlockSpec(memory_space=pltpu.VMEM)],
        out_specs=pl.BlockSpec(memory_space=pl.ANY),
        scratch_shapes=[
            pltpu.VMEM((9, F, LANES), jnp.float32),
            pltpu.SemaphoreType.DMA((4,)),
        ],
        compiler_params=pltpu.CompilerParams(vmem_limit_bytes=28 * 2**20),
        cost_estimate=pl.CostEstimate(flops=0, bytes_accessed=12 * 2**20, transcendentals=0),
        name="spectra_rows",
    )(transforms)


def sum_over(value, axes):
    count = lax.axis_size(axes)
    copies = jnp.broadcast_to(value[None], (count, *value.shape))
    return jnp.sum(lax.all_to_all(copies, axes, 0, 0, tiled=True), axis=0)


def on_device(velocity, starts, picks):
    times, comps, points = velocity.shape
    x = jnp.transpose(velocity, (1, 0, 2)).reshape(comps * times, points)
    chosen = gather_points(picks, x)
    arrived = lax.all_to_all(chosen, DEV, 0, 0, tiled=True)
    transforms, own = window_transforms(starts, arrived, points)
    spectra = spectra_rows(transforms)
    return (spectra, sum_over(sum_over(own, ("xl", "y")), "z"))


def solution(mesh):
    fine = Mesh(mesh.devices.reshape(4, 8, 2, 8), ("grp", *DEV))
    return jax.shard_map(
        on_device,
        mesh=fine,
        in_specs=(P(DEV, None, "grp"), P(), P()),
        out_specs=(P(None, None, ("grp", *DEV)), P("grp", None)),
        check_vma=False,
    )
```

time: 706 us -> 102 us (0.14)
  the two profiles are of different devices: /device:TPU:4 before, /device:TPU:6 now
where the time goes in v1:
time: 102 us; the launch traced here: 101 us
  blocking collectives  72.6 us (71%)
  Pallas kernels  16.9 us (17%)
  waiting for transfers between devices  6.61 us (6%)
  starting transfers between devices  3.32 us (3%)
    all_to_all x1, blocking collectives, on_device(): arrived = lax.all_to_all(chosen, DEV, 0, 0, tiled=True)  59.5 us
    all_to_all x1, blocking collectives, sum_over(): return jnp.sum(lax.all_to_all(copies, axes, 0, 0, tiled=True), axis=0)  13.1 us
    pallas_call x1, Pallas kernels, gather_points(): pl.pallas_call(gather_kernel, out_shape=jax.ShapeDtypeStruct((blocks, row...  12.5 us
    all_to_all x1, waiting for transfers between devices, sum_over(): return jnp.sum(lax.all_to_all(copies, axes, 0, 0, tiled=True), axis=0)  6.61 us
    all_to_all x1, starting transfers between devices, sum_over(): return jnp.sum(lax.all_to_all(copies, axes, 0, 0, tiled=True), axis=0)  3.32 us
    pallas_call x1, Pallas kernels, window_transforms(): pl.pallas_call(functools.partial(transforms_kernel, points), out_shape=(j...  3.04 us
  transfers between devices with their start and end apart: 1, of which 1 were waited for; matrix products, arithmetic and copies ran while one was open for 0% of the time, Pallas kernels for 1%

profile of v1, /device:TPU:6, one launch (start us, length us, event | category | flops | bytes accessed | tf_op | source)
XLA Modules:
  0.0 101.4 jit_solution(13176760546682120913)
XLA Ops:
  0.6 12.5 %gather_points.1 = f32[128,24,128]{2,1,0:T(8,128)} custom-call(s32[128,128]{1,0:T(8,128)} %bitcast.5, f32[24,16384]{1,0:T(8,128)} %bitcast.4), custom_call_target="tpu_custom_call" | custom-call | tf_op jit(solution)/shard_map/gather_points/pallas_call | solution.py:161
  13.1 0.0 copy-start
  13.1 0.0 copy-start.1
  13.2 0.0 copy-start.2
  13.2 0.0 copy-start.3
  13.2 59.5 %all_to_all.15.x_ref = f32[128,24,128]{2,1,0:T(8,128)S(1)} all-to-all(f32[128,24,128]{2,1,0:T(8,128)} %gather_points.1), channel_id=1, replica_groups=mesh['grp'=4,'z'=8,'xl'=2,'y'=8] {'z','xl','y'}, dimensions={0} | all-to-all | bytes 3145728 | tf_op jit(solution)/shard_map/all_to_all | solution.py:313
  72.7 0.0 copy-done
  72.7 0.0 copy-done.1
  72.7 0.0 copy-done.2
  72.7 0.0 copy-done.3
  72.7 3.0 %window_transforms.1 = (f32[3,2,256,384]{3,2,1,0:T(8,128)S(1)}, f32[3,256]{1,0:T(4,128)S(1)}) custom-call(s32[3]{0:T(128)S(1)} %copy-done.3, f32[128,24,128]{2,1,0:T(8,128)S(1)} %all_to_all.15.x_ref, bf16[2,256,256]{2,1,0:T(8,128)(2,1)S(1)} %copy-done.2, bf16[2,256,256]{2,1,0:T(8,128)(2,1)S(1)} %copy-done.1, f32[2,512,128]{2,1,0:T(8,128)S(1)} %copy-done), custom_call_target="tpu_custom_call" | custom-call | tf_op jit(solution)/shard_map/window_transforms/pallas_call | solution.py:273
  75.8 13.1 %all_to_all.16 = f32[16,3,256]{2,1,0:T(4,128)S(1)} all-to-all(f32[16,3,256]{2,1,0:T(4,128)S(1)} %broadcast_in_dim.4), channel_id=1, replica_groups=mesh['grp'=4,'z'=8,'xl'=2,'y'=8] {'xl','y'}, dimensions={0} | all-to-all | bytes 98304 | tf_op jit(solution)/shard_map/all_to_all | solution.py:306
  88.9 0.6 broadcast_in_dim.5
  89.6 3.3 %all-to-all-start.2 = ((f32[8,3,256]{2,1,0:T(4,128)}), f32[8,3,256]{2,1,0:T(4,128)S(1)}, u32[]{:S(2)}, u32[]{:S(2)}) async-start(f32[8,3,256]{2,1,0:T(4,128)} %broadcast_in_dim.5), calls=%async_computation.2 | async-start | bytes 65536 | tf_op jit(solution)/shard_map/all_to_all | solution.py:306
  92.9 1.3 %spectra_rows.1 = f32[9,256,128]{2,1,0:T(8,128)} custom-call(f32[3,2,256,384]{3,2,1,0:T(8,128)S(1)} %get-tuple-element.4.res_ref), custom_call_target="tpu_custom_call" | custom-call | bytes 12582912 | tf_op jit(solution)/shard_map/spectra_rows/pallas_call | solution.py:288
  94.2 6.6 %all-to-all-done.2 = f32[8,3,256]{2,1,0:T(4,128)S(1)} async-done(((f32[8,3,256]{2,1,0:T(4,128)}), f32[8,3,256]{2,1,0:T(4,128)S(1)}, u32[]{:S(2)}, u32[]{:S(2)}) %all-to-all-start.2) | async-done | bytes 24608 | tf_op jit(solution)/shard_map/all_to_all | solution.py:306
  100.8 0.6 reduce_sum.19
  (2 shorter events, 0.1 us)
Async XLA Ops:
  13.1 59.6 %copy-start = (f32[2,512,128]{2,1,0:T(8,128)S(1)}, f32[2,512,128]{2,1,0:T(8,128)}, u32[]{:S(2)}) copy-start(f32[2,512,128]{2,1,0:T(8,128)} %constant.10.clone.turns_ref) | copy-start | bytes 1572868
  13.1 59.5 %copy-start.1 = (bf16[2,256,256]{2,1,0:T(8,128)(2,1)S(1)}, bf16[2,256,256]{2,1,0:T(8,128)(2,1)}, u32[]{:S(2)}) copy-start(bf16[2,256,256]{2,1,0:T(8,128)(2,1)} %constant.9.clone.low_ref) | copy-start | bytes 786436
  13.2 59.5 %copy-start.2 = (bf16[2,256,256]{2,1,0:T(8,128)(2,1)S(1)}, bf16[2,256,256]{2,1,0:T(8,128)(2,1)}, u32[]{:S(2)}) copy-start(bf16[2,256,256]{2,1,0:T(8,128)(2,1)} %constant.8.clone.high_ref) | copy-start | bytes 786436
  13.2 59.5 %copy-start.3 = (s32[3]{0:T(128)S(1)}, s32[3]{0:T(128)}, u32[]{:S(2)}) copy-start(s32[3]{0:T(128)} %starts_ref.1) | copy-start | bytes 40
  89.6 11.3 %all-to-all-start.2 = ((f32[8,3,256]{2,1,0:T(4,128)}), f32[8,3,256]{2,1,0:T(4,128)S(1)}, u32[]{:S(2)}, u32[]{:S(2)}) async-start(f32[8,3,256]{2,1,0:T(4,128)} %broadcast_in_dim.5), calls=%async_computation.2 | async-start | bytes 65536 | tf_op jit(solution)/shard_map/all_to_all | solution.py:306

commit v2 on v1

--- a/solution.py
+++ b/solution.py
@@ -17,32 +17,28 @@
 DEV = ("z", "xl", "y")
 
 
-def split_bf16(table):
-    high = table.astype(ml_dtypes.bfloat16)
-    low = (table - high.astype(np.float64)).astype(ml_dtypes.bfloat16)
-    return high, low
-
-
 def make_tables():
     half = np.arange(L // 2)
     bins = np.arange(F // 2)
     bases = []
     for odd in (0, 1):
         phase = ((2 * bins[:, None] + odd) * half[None, :] % L) * (2.0 * np.pi / L)
-        bases.append(np.concatenate([np.cos(phase), -np.sin(phase)], axis=0))
-    high, low = split_bf16(np.stack(bases))
+        basis = np.concatenate([np.cos(phase), -np.sin(phase)], axis=0)
+        high = basis.astype(ml_dtypes.bfloat16)
+        low = (basis - high.astype(np.float64)).astype(ml_dtypes.bfloat16)
+        bases.append(np.concatenate([high, high, low], axis=1))
     turn = np.arange(L) * (2.0 * np.pi / L)
-    turns = np.stack([np.cos(turn), np.sin(turn)]).astype(np.float32)
-    turns = np.broadcast_to(turns[:, :, None], (2, L, LANES))
     taper = 0.5 - 0.5 * np.cos(turn)
-    return high, low, np.ascontiguousarray(turns), float(1.0 / (np.sum(taper * taper) * W))
-
-
-BASIS_HIGH, BASIS_LOW, TURNS, SCALE = make_tables()
+    turns = np.stack([np.cos(turn), np.sin(turn), taper]).astype(np.float32)
+    turns = np.ascontiguousarray(np.broadcast_to(turns[:, :, None], (3, L, LANES)))
+    return np.stack(bases), turns, float(1.0 / (np.sum(taper * taper) * W))
+
+
+BASES, TURNS, SCALE = make_tables()
 
 
 def gather_kernel(
-    picks_ref, x_ref, out_ref, picks, x, table, index, even, odd, out, sems, index_sems, x_sems, out_sems
+    picks_ref, x_ref, out_ref, picks, x, table, index, which, even, odd, out, sems, index_sems, x_sems, out_sems
 ):
     rows, points = x.shape
     blocks = out.shape[0]
@@ -58,15 +54,13 @@
     picks_copy.start()
     x_copies = []
     for piece in range(pieces):
-        for q in range(QUARTERS):
-            span = pl.ds(q * quarter + piece * width, width)
-            x_copies.append(
-                pltpu.make_async_copy(x_ref.at[:, span], x.at[:, span], x_sems.at[piece, q])
-            )
-    for copy in x_copies:
-        copy.start()
+        span = pl.ds(piece * width * QUARTERS, width * QUARTERS)
+        x_copies.append(pltpu.make_async_copy(x_ref.at[:, span], x.at[:, span], x_sems.at[piece]))
+        x_copies[piece].start()
     picks_copy.wait()
-    index[...] = picks[...] % quarter
+    source = picks[...] // LANES
+    index[...] = source // QUARTERS * LANES + picks[...] % LANES
+    which[...] = source % QUARTERS
 
     def index_copy(slot, first):
         held = (even, odd)[slot]
@@ -76,16 +70,14 @@
     index_copy(1, together).start()
 
     pad = jnp.zeros((apart - rows, LANES), jnp.float32)
-    for piece in range(pieces):
-        for copy in x_copies[piece * QUARTERS : (piece + 1) * QUARTERS]:
-            copy.wait()
-
-        for block in range(width // LANES):
-            start = piece * width + block * LANES
-            parts = []
-            for q in range(QUARTERS):
-                parts += [x[:, q * quarter + start : q * quarter + start + LANES], pad]
-            table[start : start + LANES, :] = jnp.concatenate(parts, axis=0).T
+    for copy in x_copies:
+        copy.wait()
+    for block in range(quarter // LANES):
+        parts = []
+        for q in range(QUARTERS):
+            start = (block * QUARTERS + q) * LANES
+            parts += [x[:, start : start + LANES], pad]
+        table[block * LANES : (block + 1) * LANES, :] = jnp.concatenate(parts, axis=0).T
 
     point_rows = table.reshape(quarter, 1, LANES)
     row = lax.broadcasted_iota(jnp.int32, (8, LANES), 0)
@@ -106,11 +98,11 @@
         return jnp.concatenate(tiles, axis=0)
 
     def keep(block, turned):
-        which = jnp.broadcast_to(picks[pl.ds(block, 1), :], (rows, LANES))
+        chosen = jnp.broadcast_to(which[pl.ds(block, 1), :], (rows, LANES))
         value = turned[0:rows]
         for q in range(1, QUARTERS):
             part = turned[q * apart : q * apart + rows]
-            value = jnp.where(which >= q * quarter, part, value)
+            value = jnp.where(chosen == q, part, value)
         out[block] = value
 
     def batch(held, first, before):
@@ -168,33 +160,42 @@
             vmem((rows, points), jnp.float32),
             vmem((points // QUARTERS, LANES), jnp.float32),
             vmem((blocks, LANES), jnp.int32),
-            pltpu.SMEM((8, LANES), jnp.int32),
-            pltpu.SMEM((8, LANES), jnp.int32),
+            vmem((blocks, LANES), jnp.int32),
+            pltpu.SMEM((16, LANES), jnp.int32),
+            pltpu.SMEM((16, LANES), jnp.int32),
             vmem((blocks, rows, LANES), jnp.float32),
             pltpu.SemaphoreType.DMA((1,)),
             pltpu.SemaphoreType.DMA((2,)),
-            pltpu.SemaphoreType.DMA((pieces, QUARTERS)),
-            pltpu.SemaphoreType.DMA((8,)),
+            pltpu.SemaphoreType.DMA((pieces,)),
+            pltpu.SemaphoreType.DMA((4,)),
         ],
         compiler_params=pltpu.CompilerParams(vmem_limit_bytes=58 * 2**20),
         name="gather_points",
     )(picks.reshape(blocks, LANES), x)
 
 
-def transforms_kernel(points, starts_ref, x_ref, high_ref, low_ref, turns_ref, res_ref, own_ref, power_ref):
+def transforms_kernel(points, starts_ref, x_ref, bases_ref, turns_ref, res_ref, own_ref, power_ref):
     half = L // 2
     sample = lax.broadcasted_iota(jnp.int32, (L, LANES), 0)
     for w in range(W):
-        start = starts_ref[w]
-        turn = lax.rem(start, L)
-        cos_start = turns_ref[0, pl.ds(turn, 1), :]
-        sin_start = turns_ref[1, pl.ds(turn, 1), :]
-        taper = 0.5 - 0.5 * (turns_ref[0] * cos_start + turns_ref[1] * sin_start)
-        late = sample >= start
+        if 0 < w < W - 1:
+            start = starts_ref[w]
+            turn = lax.rem(start, L)
+            cos_start = turns_ref[0, pl.ds(turn, 1), :]
+            sin_start = turns_ref[1, pl.ds(turn, 1), :]
+            taper = 0.5 - 0.5 * (turns_ref[0] * cos_start + turns_ref[1] * sin_start)
+            late = sample >= start
+        else:
+            taper = turns_ref[2]
         terms = [[], []]
         for comp in range(3):
             series = x_ref[:, comp * 8 : comp * 8 + 8, :].reshape(2 * L, LANES)
-            frame = jnp.where(late, series[0:L], series[L : 2 * L])
+            if w == 0:
+                frame = series[0:L]
+            elif w == W - 1:
+                frame = series[L : 2 * L]
+            else:
+                frame = jnp.where(late, series[0:L], series[L : 2 * L])
             centred = frame - jnp.sum(frame, axis=0, keepdims=True) * (1.0 / L)
             tapered = centred * taper
             terms[0].append(tapered[0:half] + tapered[half:L])
@@ -203,9 +204,10 @@
             term = jnp.concatenate(terms[odd], axis=1)
             high = term.astype(jnp.bfloat16)
             low = (term - high.astype(jnp.float32)).astype(jnp.bfloat16)
-            dot = functools.partial(jnp.dot, preferred_element_type=jnp.float32)
-            res_ref[w, odd] = (
-                dot(high_ref[odd], high) + dot(high_ref[odd], low) + dot(low_ref[odd], high)
+            res_ref[w, odd] = jnp.dot(
+                bases_ref[odd],
+                jnp.concatenate([high, low, high], axis=0),
+                preferred_element_type=jnp.float32,
             )
 
     for odd in (0, 1):
@@ -216,16 +218,20 @@
         for comp in range(3):
             span = slice(comp * LANES, (comp + 1) * LANES)
             power_ref[comp, pl.ds(odd, F // 2, stride=2), :] = power[:, span]
-    ones = jnp.ones((8, LANES), jnp.float32)
+    ones = jnp.ones((16, LANES), jnp.bfloat16)
     for comp in range(3):
-        sums = lax.dot_general(
-            ones,
-            power_ref[comp],
-            (((1,), (1,)), ((), ())),
-            precision=lax.Precision.HIGHEST,
-            preferred_element_type=jnp.float32,
-        )
-        own_ref[comp : comp + 1, :] = sums[0:1] * (SCALE / points)
+        power = power_ref[comp]
+        high = power.astype(jnp.bfloat16)
+        low = (power - high.astype(jnp.float32)).astype(jnp.bfloat16)
+        sums = [
+            lax.dot_general(
+                ones, term, (((1,), (1,)), ((), ())), preferred_element_type=jnp.float32
+            )[0:1]
+            for term in (high, low)
+        ]
+        share = (sums[0] + sums[1]) * (SCALE / points)
+        for copy in range(own_ref.shape[0]):
+            own_ref[copy, :, comp * F : (comp + 1) * F] = share
 
 
 def rows_kernel(res_ref, spectra_ref, out_ref, out_sems):
@@ -268,20 +274,20 @@
         copy.wait()
 
 
-def window_transforms(starts, arrived, points):
+def window_transforms(starts, arrived, points, copies):
     vmem = pl.BlockSpec(memory_space=pltpu.VMEM)
     return pl.pallas_call(
         functools.partial(transforms_kernel, points),
         out_shape=(
             jax.ShapeDtypeStruct((W, 2, F, 3 * LANES), jnp.float32),
-            jax.ShapeDtypeStruct((3, F), jnp.float32),
+            jax.ShapeDtypeStruct((copies, 1, 3 * F), jnp.float32),
         ),
-        in_specs=[pl.BlockSpec(memory_space=pltpu.SMEM)] + [vmem] * 4,
+        in_specs=[pl.BlockSpec(memory_space=pltpu.SMEM)] + [vmem] * 3,
         out_specs=(vmem, vmem),
         scratch_shapes=[pltpu.VMEM((3, F, LANES), jnp.float32)],
         compiler_params=pltpu.CompilerParams(vmem_limit_bytes=28 * 2**20),
         name="window_transforms",
-    )(starts, arrived, jnp.asarray(BASIS_HIGH), jnp.asarray(BASIS_LOW), jnp.asarray(TURNS))
+    )(starts, arrived, jnp.asarray(BASES), jnp.asarray(TURNS))
 
 
 def spectra_rows(transforms):
@@ -300,20 +306,16 @@
     )(transforms)
 
 
-def sum_over(value, axes):
-    count = lax.axis_size(axes)
-    copies = jnp.broadcast_to(value[None], (count, *value.shape))
-    return jnp.sum(lax.all_to_all(copies, axes, 0, 0, tiled=True), axis=0)
-
-
 def on_device(velocity, starts, picks):
     times, comps, points = velocity.shape
     x = jnp.transpose(velocity, (1, 0, 2)).reshape(comps * times, points)
     chosen = gather_points(picks, x)
     arrived = lax.all_to_all(chosen, DEV, 0, 0, tiled=True)
-    transforms, own = window_transforms(starts, arrived, points)
+    plane = ("z", "y")
+    transforms, copies = window_transforms(starts, arrived, points, lax.axis_size(plane))
     spectra = spectra_rows(transforms)
-    return (spectra, sum_over(sum_over(own, ("xl", "y")), "z"))
+    total = jnp.sum(lax.all_to_all(copies, plane, 0, 0, tiled=True), axis=0)
+    return (spectra, lax.psum(total.reshape(3, F), "xl"))
 
 
 def solution(mesh):

time: 102 us -> 101 us (level)
  blocking collectives: 72.6 us -> 65 us
  waiting for transfers between devices: 6.61 us -> 12.6 us
  starting transfers between devices: 3.32 us -> 5.77 us
    all_to_all x1 -> x0, blocking collectives: 13.1 us -> none  [sum_over(): return jnp.sum(lax.all_to_all(copies, axes, 0, 0, tiled=True), axis=0)]
    all_to_all x1, waiting for transfers between devices: 6.61 us -> 12.6 us  [on_device(): total = jnp.sum(lax.all_to_all(copies, plane, 0, 0, tiled=True), axis=0)]
    psum x0 -> x1, blocking collectives: none -> 5.53 us  [on_device(): return (spectra, lax.psum(total.reshape(3, F), 'xl'))]
    all_to_all x1, starting transfers between devices: 3.32 us -> 5.77 us  [on_device(): total = jnp.sum(lax.all_to_all(copies, plane, 0, 0, tiled=True), axis=0)]
where the time goes in v2:
time: 101 us
  blocking collectives  65 us (64%)
  Pallas kernels  16.5 us (16%)
  waiting for transfers between devices  12.6 us (12%)
  starting transfers between devices  5.77 us (6%)
    all_to_all x1, blocking collectives, on_device(): arrived = lax.all_to_all(chosen, DEV, 0, 0, tiled=True)  59.5 us
    all_to_all x1, waiting for transfers between devices, on_device(): total = jnp.sum(lax.all_to_all(copies, plane, 0, 0, tiled=True), axis=0)  12.6 us
    pallas_call x1, Pallas kernels, gather_points(): pl.pallas_call(gather_kernel, out_shape=jax.ShapeDtypeStruct((blocks, row...  11.9 us
    all_to_all x1, starting transfers between devices, on_device(): total = jnp.sum(lax.all_to_all(copies, plane, 0, 0, tiled=True), axis=0)  5.77 us
    psum x1, blocking collectives, on_device(): return (spectra, lax.psum(total.reshape(3, F), 'xl'))  5.53 us
    pallas_call x1, Pallas kernels, window_transforms(): pl.pallas_call(functools.partial(transforms_kernel, points), out_shape=(j...  3.22 us
  transfers between devices with their start and end apart: 1, of which 1 were waited for; matrix products, arithmetic and copies ran while one was open for 0% of the time, Pallas kernels for 1%

profile of v2, /device:TPU:6, one launch (start us, length us, event | category | flops | bytes accessed | tf_op | source)
XLA Modules:
  0.0 100.7 jit_solution(14268120207062857463)
XLA Ops:
  0.6 11.9 %gather_points.1 = f32[128,24,128]{2,1,0:T(8,128)} custom-call(s32[128,128]{1,0:T(8,128)} %bitcast.5, f32[24,16384]{1,0:T(8,128)} %bitcast.4), custom_call_target="tpu_custom_call" | custom-call | tf_op jit(solution)/shard_map/gather_points/pallas_call | solution.py:153
  12.6 0.0 copy-start
  12.6 0.0 copy-start.1
  12.6 0.0 copy-start.2
  12.6 59.5 %all_to_all.10.x_ref = f32[128,24,128]{2,1,0:T(8,128)S(1)} all-to-all(f32[128,24,128]{2,1,0:T(8,128)} %gather_points.1), channel_id=1, replica_groups=mesh['grp'=4,'z'=8,'xl'=2,'y'=8] {'z','xl','y'}, dimensions={0} | all-to-all | bytes 3145728 | tf_op jit(solution)/shard_map/all_to_all | solution.py:313
  72.1 0.0 copy-done
  72.1 0.0 copy-done.1
  72.1 0.0 copy-done.2
  72.1 3.2 %window_transforms.1 = (f32[3,2,256,384]{3,2,1,0:T(8,128)S(1)}, f32[64,1,768]{2,1,0:T(1,128)}) custom-call(s32[3]{0:T(128)S(1)} %copy-done.2, f32[128,24,128]{2,1,0:T(8,128)S(1)} %all_to_all.10.x_ref, bf16[2,256,768]{2,1,0:T(8,128)(2,1)S(1)} %copy-done.1, f32[3,512,128]{2,1,0:T(8,128)S(1)} %copy-done), custom_call_target="tpu_custom_call" | custom-call | tf_op jit(solution)/shard_map/window_transforms/pallas_call | solution.py:279
  75.3 5.8 %all-to-all-start.1 = ((f32[64,1,768]{2,1,0:T(1,128)}), f32[64,1,768]{2,1,0:T(1,128)S(1)}, u32[]{:S(2)}, u32[]{:S(2)}) async-start(f32[64,1,768]{2,1,0:T(1,128)} %get-tuple-element.5), calls=%async_computation.1 | async-start | bytes 393216 | tf_op jit(solution)/shard_map/all_to_all | solution.py:317
  81.1 1.3 %spectra_rows.1 = f32[9,256,128]{2,1,0:T(8,128)} custom-call(f32[3,2,256,384]{3,2,1,0:T(8,128)S(1)} %get-tuple-element.4.res_ref), custom_call_target="tpu_custom_call" | custom-call | bytes 12582912 | tf_op jit(solution)/shard_map/spectra_rows/pallas_call | solution.py:294
  82.4 12.6 %all-to-all-done.1 = f32[64,1,768]{2,1,0:T(1,128)S(1)} async-done(((f32[64,1,768]{2,1,0:T(1,128)}), f32[64,1,768]{2,1,0:T(1,128)S(1)}, u32[]{:S(2)}, u32[]{:S(2)}) %all-to-all-start.1) | async-done | bytes 196640 | tf_op jit(solution)/shard_map/all_to_all | solution.py:317
  95.0 0.1 reduce_sum.9
  95.2 5.5 %psum.7 = f32[3,256]{1,0:T(4,128)} all-reduce(f32[3,256]{1,0:T(4,128)S(1)} %reshape.17), channel_id=1, replica_groups=mesh['grp'=4,'z'=8,'xl'=2,'y'=8] {'xl'}, use_global_device_ids=true, to_apply=%region_1.0 | all-reduce | flops 768 | bytes 6144 | tf_op jit(solution)/shard_map/psum | solution.py:318
  (1 shorter events, 0.0 us)
Async XLA Ops:
  12.6 59.5 %copy-start = (f32[3,512,128]{2,1,0:T(8,128)S(1)}, f32[3,512,128]{2,1,0:T(8,128)}, u32[]{:S(2)}) copy-start(f32[3,512,128]{2,1,0:T(8,128)} %constant.7.clone.turns_ref) | copy-start | bytes 2359300
  12.6 59.5 %copy-start.1 = (bf16[2,256,768]{2,1,0:T(8,128)(2,1)S(1)}, bf16[2,256,768]{2,1,0:T(8,128)(2,1)}, u32[]{:S(2)}) copy-start(bf16[2,256,768]{2,1,0:T(8,128)(2,1)} %constant.6.clone.bases_ref) | copy-start | bytes 2359300
  12.6 59.5 %copy-start.2 = (s32[3]{0:T(128)S(1)}, s32[3]{0:T(128)}, u32[]{:S(2)}) copy-start(s32[3]{0:T(128)} %starts_ref.1) | copy-start | bytes 40
  75.3 19.7 %all-to-all-start.1 = ((f32[64,1,768]{2,1,0:T(1,128)}), f32[64,1,768]{2,1,0:T(1,128)S(1)}, u32[]{:S(2)}, u32[]{:S(2)}) async-start(f32[64,1,768]{2,1,0:T(1,128)} %get-tuple-element.5), calls=%async_computation.1 | async-start | bytes 393216 | tf_op jit(solution)/shard_map/all_to_all | solution.py:317

commit v3 on v2

--- a/solution.py
+++ b/solution.py
@@ -177,6 +177,7 @@
 def transforms_kernel(points, starts_ref, x_ref, bases_ref, turns_ref, res_ref, own_ref, power_ref):
     half = L // 2
     sample = lax.broadcasted_iota(jnp.int32, (L, LANES), 0)
+    stacked = [[], []]
     for w in range(W):
         if 0 < w < W - 1:
             start = starts_ref[w]
@@ -204,21 +205,23 @@
             term = jnp.concatenate(terms[odd], axis=1)
             high = term.astype(jnp.bfloat16)
             low = (term - high.astype(jnp.float32)).astype(jnp.bfloat16)
-            res_ref[w, odd] = jnp.dot(
-                bases_ref[odd],
-                jnp.concatenate([high, low, high], axis=0),
-                preferred_element_type=jnp.float32,
-            )
+            stacked[odd].append(jnp.concatenate([high, low, high], axis=0))
 
     for odd in (0, 1):
         power = jnp.zeros((F // 2, 3 * LANES), jnp.float32)
         for w in range(W):
-            real, imag = res_ref[w, odd, 0 : F // 2, :], res_ref[w, odd, F // 2 : F, :]
+            result = jnp.dot(
+                bases_ref[odd], stacked[odd][w], preferred_element_type=jnp.float32
+            )
+            res_ref[w, odd] = result
+            real, imag = result[0 : F // 2], result[F // 2 : F]
             power += real * real + imag * imag
         for comp in range(3):
             span = slice(comp * LANES, (comp + 1) * LANES)
             power_ref[comp, pl.ds(odd, F // 2, stride=2), :] = power[:, span]
+
     ones = jnp.ones((16, LANES), jnp.bfloat16)
+    shares = []
     for comp in range(3):
         power = power_ref[comp]
         high = power.astype(jnp.bfloat16)
@@ -226,12 +229,22 @@
         sums = [
             lax.dot_general(
                 ones, term, (((1,), (1,)), ((), ())), preferred_element_type=jnp.float32
-            )[0:1]
+            )[0:8]
             for term in (high, low)
         ]
         share = (sums[0] + sums[1]) * (SCALE / points)
-        for copy in range(own_ref.shape[0]):
-            own_ref[copy, :, comp * F : (comp + 1) * F] = share
+        shares += [share[:, 0:LANES], share[:, LANES:F]]
+    row = lax.broadcasted_iota(jnp.int32, (8, LANES), 0)
+    tiles = []
+    for tile in range(3):
+        place = lax.rem(row + 8 * tile, len(shares))
+        value = shares[0]
+        for i in range(1, len(shares)):
+            value = jnp.where(place == i, shares[i], value)
+        tiles.append(value)
+    pattern = jnp.concatenate(tiles, axis=0)
+    for first in range(0, own_ref.shape[0], 24):
+        own_ref[first : first + 24, :] = pattern
 
 
 def rows_kernel(res_ref, spectra_ref, out_ref, out_sems):
@@ -280,7 +293,7 @@
         functools.partial(transforms_kernel, points),
         out_shape=(
             jax.ShapeDtypeStruct((W, 2, F, 3 * LANES), jnp.float32),
-            jax.ShapeDtypeStruct((copies, 1, 3 * F), jnp.float32),
+            jax.ShapeDtypeStruct((copies * 3 * F // LANES, LANES), jnp.float32),
         ),
         in_specs=[pl.BlockSpec(memory_space=pltpu.SMEM)] + [vmem] * 3,
         out_specs=(vmem, vmem),
@@ -314,8 +327,10 @@
     plane = ("z", "y")
     transforms, copies = window_transforms(starts, arrived, points, lax.axis_size(plane))
     spectra = spectra_rows(transforms)
+    copies = copies.reshape(-1, 3, F // LANES, LANES)
     total = jnp.sum(lax.all_to_all(copies, plane, 0, 0, tiled=True), axis=0)
-    return (spectra, lax.psum(total.reshape(3, F), "xl"))
+    total = jnp.sum(lax.all_gather(total, "xl"), axis=0)
+    return (spectra, total.reshape(3, F))
 
 
 def solution(mesh):

time: 101 us -> 100 us (0.990)
  blocking collectives: 65 us -> 63.8 us
    psum x1 -> x0, blocking collectives: 5.53 us -> none  [on_device(): return (spectra, lax.psum(total.reshape(3, F), 'xl'))]
    all_gather x0 -> x1, blocking collectives: none -> 4.33 us  [on_device(): total = jnp.sum(lax.all_gather(total, 'xl'), axis=0)]
where the time goes in v3:
time: 100 us
  blocking collectives  63.8 us (64%)
  Pallas kernels  16.5 us (16%)
  waiting for transfers between devices  12.6 us (13%)
  starting transfers between devices  5.76 us (6%)
    all_to_all x1, blocking collectives, on_device(): arrived = lax.all_to_all(chosen, DEV, 0, 0, tiled=True)  59.5 us
    all_to_all x1, waiting for transfers between devices, on_device(): total = jnp.sum(lax.all_to_all(copies, plane, 0, 0, tiled=True), axis=0)  12.6 us
    pallas_call x1, Pallas kernels, gather_points(): pl.pallas_call(gather_kernel, out_shape=jax.ShapeDtypeStruct((blocks, row...  11.9 us
    all_to_all x1, starting transfers between devices, on_device(): total = jnp.sum(lax.all_to_all(copies, plane, 0, 0, tiled=True), axis=0)  5.76 us
    all_gather x1, blocking collectives, on_device(): total = jnp.sum(lax.all_gather(total, 'xl'), axis=0)  4.33 us
    pallas_call x1, Pallas kernels, window_transforms(): pl.pallas_call(functools.partial(transforms_kernel, points), out_shape=(j...  3.24 us
  transfers between devices with their start and end apart: 1, of which 1 were waited for; matrix products, arithmetic and copies ran while one was open for 0% of the time, Pallas kernels for 1%

profile of v3, /device:TPU:6, one launch (start us, length us, event | category | flops | bytes accessed | tf_op | source)
XLA Modules:
  0.0 100.0 jit_solution(2755552685404146875)
XLA Ops:
  0.6 11.9 %gather_points.1 = f32[128,24,128]{2,1,0:T(8,128)} custom-call(s32[128,128]{1,0:T(8,128)} %bitcast.11, f32[24,16384]{1,0:T(8,128)} %bitcast.10), custom_call_target="tpu_custom_call" | custom-call | tf_op jit(solution)/shard_map/gather_points/pallas_call | solution.py:153
  12.6 0.0 copy-start
  12.6 0.0 copy-start.1
  12.6 0.0 copy-start.2
  12.6 59.5 %all_to_all.10.x_ref = f32[128,24,128]{2,1,0:T(8,128)S(1)} all-to-all(f32[128,24,128]{2,1,0:T(8,128)} %gather_points.1), channel_id=1, replica_groups=mesh['grp'=4,'z'=8,'xl'=2,'y'=8] {'z','xl','y'}, dimensions={0} | all-to-all | bytes 3145728 | tf_op jit(solution)/shard_map/all_to_all | solution.py:326
  72.1 0.0 copy-done
  72.1 0.0 copy-done.1
  72.1 0.0 copy-done.2
  72.1 3.2 %window_transforms.1 = (f32[3,2,256,384]{3,2,1,0:T(8,128)S(1)}, f32[384,128]{1,0:T(8,128)}) custom-call(s32[3]{0:T(128)S(1)} %copy-done.2, f32[128,24,128]{2,1,0:T(8,128)S(1)} %all_to_all.10.x_ref, bf16[2,256,768]{2,1,0:T(8,128)(2,1)S(1)} %copy-done.1, f32[3,512,128]{2,1,0:T(8,128)S(1)} %copy-done), custom_call_target="tpu_custom_call" | custom-call | tf_op jit(solution)/shard_map/window_transforms/pallas_call | solution.py:292
  75.3 5.8 %all-to-all-start.1 = ((f32[64,3,2,128]{3,2,1,0:T(2,128)}), f32[64,3,2,128]{3,2,1,0:T(2,128)S(1)}, u32[]{:S(2)}, u32[]{:S(2)}) async-start(f32[64,3,2,128]{3,2,1,0:T(2,128)} %bitcast.3), calls=%async_computation.1 | async-start | bytes 393216 | tf_op jit(solution)/shard_map/all_to_all | solution.py:331
  81.1 1.3 %spectra_rows.1 = f32[9,256,128]{2,1,0:T(8,128)} custom-call(f32[3,2,256,384]{3,2,1,0:T(8,128)S(1)} %get-tuple-element.4.res_ref), custom_call_target="tpu_custom_call" | custom-call | bytes 12582912 | tf_op jit(solution)/shard_map/spectra_rows/pallas_call | solution.py:307
  82.4 12.6 %all-to-all-done.1 = f32[64,3,2,128]{3,2,1,0:T(2,128)S(1)} async-done(((f32[64,3,2,128]{3,2,1,0:T(2,128)}), f32[64,3,2,128]{3,2,1,0:T(2,128)S(1)}, u32[]{:S(2)}, u32[]{:S(2)}) %all-to-all-start.1) | async-done | bytes 196640 | tf_op jit(solution)/shard_map/all_to_all | solution.py:331
  95.0 0.1 reduce_sum.18
  95.1 4.3 %all-gather = f32[6,2,128]{2,1,0:T(2,128)S(1)} all-gather(f32[3,2,128]{2,1,0:T(2,128)S(1)} %reduce_sum.18), channel_id=2, replica_groups=mesh['grp'=4,'z'=8,'xl'=2,'y'=8] {'xl'}, dimensions={0}, use_global_device_ids=true | all-gather | bytes 9216 | tf_op jit(solution)/shard_map/all_gather | solution.py:332
  99.4 0.6 copy.9
  (1 shorter events, 0.0 us)
Async XLA Ops:
  12.6 59.5 %copy-start = (f32[3,512,128]{2,1,0:T(8,128)S(1)}, f32[3,512,128]{2,1,0:T(8,128)}, u32[]{:S(2)}) copy-start(f32[3,512,128]{2,1,0:T(8,128)} %constant.7.clone.turns_ref) | copy-start | bytes 2359300
  12.6 59.5 %copy-start.1 = (bf16[2,256,768]{2,1,0:T(8,128)(2,1)S(1)}, bf16[2,256,768]{2,1,0:T(8,128)(2,1)}, u32[]{:S(2)}) copy-start(bf16[2,256,768]{2,1,0:T(8,128)(2,1)} %constant.6.clone.bases_ref) | copy-start | bytes 2359300
  12.6 59.5 %copy-start.2 = (s32[3]{0:T(128)S(1)}, s32[3]{0:T(128)}, u32[]{:S(2)}) copy-start(s32[3]{0:T(128)} %starts_ref.1) | copy-start | bytes 40
  75.3 19.7 %all-to-all-start.1 = ((f32[64,3,2,128]{3,2,1,0:T(2,128)}), f32[64,3,2,128]{3,2,1,0:T(2,128)S(1)}, u32[]{:S(2)}, u32[]{:S(2)}) async-start(f32[64,3,2,128]{3,2,1,0:T(2,128)} %bitcast.3), calls=%async_computation.1 | async-start | bytes 393216 | tf_op jit(solution)/shard_map/all_to_all | solution.py:331

commit v4 on v3

--- a/solution.py
+++ b/solution.py
@@ -177,7 +177,6 @@
 def transforms_kernel(points, starts_ref, x_ref, bases_ref, turns_ref, res_ref, own_ref, power_ref):
     half = L // 2
     sample = lax.broadcasted_iota(jnp.int32, (L, LANES), 0)
-    stacked = [[], []]
     for w in range(W):
         if 0 < w < W - 1:
             start = starts_ref[w]
@@ -205,16 +204,16 @@
             term = jnp.concatenate(terms[odd], axis=1)
             high = term.astype(jnp.bfloat16)
             low = (term - high.astype(jnp.float32)).astype(jnp.bfloat16)
-            stacked[odd].append(jnp.concatenate([high, low, high], axis=0))
+            res_ref[w, odd] = jnp.dot(
+                bases_ref[odd],
+                jnp.concatenate([high, low, high], axis=0),
+                preferred_element_type=jnp.float32,
+            )
 
     for odd in (0, 1):
         power = jnp.zeros((F // 2, 3 * LANES), jnp.float32)
         for w in range(W):
-            result = jnp.dot(
-                bases_ref[odd], stacked[odd][w], preferred_element_type=jnp.float32
-            )
-            res_ref[w, odd] = result
-            real, imag = result[0 : F // 2], result[F // 2 : F]
+            real, imag = res_ref[w, odd, 0 : F // 2, :], res_ref[w, odd, F // 2 : F, :]
             power += real * real + imag * imag
         for comp in range(3):
             span = slice(comp * LANES, (comp + 1) * LANES)

time: 100 us -> 100 us (level)
  no operation moved by 1% of the time
where the time goes in v4:
time: 100 us
  blocking collectives  63.8 us (64%)
  Pallas kernels  16.5 us (16%)
  waiting for transfers between devices  12.6 us (13%)
  starting transfers between devices  5.77 us (6%)
    all_to_all x1, blocking collectives, on_device(): arrived = lax.all_to_all(chosen, DEV, 0, 0, tiled=True)  59.5 us
    all_to_all x1, waiting for transfers between devices, on_device(): total = jnp.sum(lax.all_to_all(copies, plane, 0, 0, tiled=True), axis=0)  12.6 us
    pallas_call x1, Pallas kernels, gather_points(): pl.pallas_call(gather_kernel, out_shape=jax.ShapeDtypeStruct((blocks, row...  11.9 us
    all_to_all x1, starting transfers between devices, on_device(): total = jnp.sum(lax.all_to_all(copies, plane, 0, 0, tiled=True), axis=0)  5.77 us
    all_gather x1, blocking collectives, on_device(): total = jnp.sum(lax.all_gather(total, 'xl'), axis=0)  4.33 us
    pallas_call x1, Pallas kernels, window_transforms(): pl.pallas_call(functools.partial(transforms_kernel, points), out_shape=(j...  3.21 us
  transfers between devices with their start and end apart: 1, of which 1 were waited for; matrix products, arithmetic and copies ran while one was open for 0% of the time, Pallas kernels for 1%

profile of v4, /device:TPU:6, one launch (start us, length us, event | category | flops | bytes accessed | tf_op | source)
XLA Modules:
  0.0 100.0 jit_solution(2093730330318290932)
XLA Ops:
  0.6 11.9 %gather_points.1 = f32[128,24,128]{2,1,0:T(8,128)} custom-call(s32[128,128]{1,0:T(8,128)} %bitcast.11, f32[24,16384]{1,0:T(8,128)} %bitcast.10), custom_call_target="tpu_custom_call" | custom-call | tf_op jit(solution)/shard_map/gather_points/pallas_call | solution.py:153
  12.6 0.0 copy-start
  12.6 0.0 copy-start.1
  12.6 0.0 copy-start.2
  12.6 59.5 %all_to_all.10.x_ref = f32[128,24,128]{2,1,0:T(8,128)S(1)} all-to-all(f32[128,24,128]{2,1,0:T(8,128)} %gather_points.1), channel_id=1, replica_groups=mesh['grp'=4,'z'=8,'xl'=2,'y'=8] {'z','xl','y'}, dimensions={0} | all-to-all | bytes 3145728 | tf_op jit(solution)/shard_map/all_to_all | solution.py:325
  72.1 0.0 copy-done
  72.1 0.0 copy-done.1
  72.1 0.0 copy-done.2
  72.1 3.2 %window_transforms.1 = (f32[3,2,256,384]{3,2,1,0:T(8,128)S(1)}, f32[384,128]{1,0:T(8,128)}) custom-call(s32[3]{0:T(128)S(1)} %copy-done.2, f32[128,24,128]{2,1,0:T(8,128)S(1)} %all_to_all.10.x_ref, bf16[2,256,768]{2,1,0:T(8,128)(2,1)S(1)} %copy-done.1, f32[3,512,128]{2,1,0:T(8,128)S(1)} %copy-done), custom_call_target="tpu_custom_call" | custom-call | tf_op jit(solution)/shard_map/window_transforms/pallas_call | solution.py:291
  75.3 5.8 %all-to-all-start.1 = ((f32[64,3,2,128]{3,2,1,0:T(2,128)}), f32[64,3,2,128]{3,2,1,0:T(2,128)S(1)}, u32[]{:S(2)}, u32[]{:S(2)}) async-start(f32[64,3,2,128]{3,2,1,0:T(2,128)} %bitcast.3), calls=%async_computation.1 | async-start | bytes 393216 | tf_op jit(solution)/shard_map/all_to_all | solution.py:330
  81.1 1.3 %spectra_rows.1 = f32[9,256,128]{2,1,0:T(8,128)} custom-call(f32[3,2,256,384]{3,2,1,0:T(8,128)S(1)} %get-tuple-element.4.res_ref), custom_call_target="tpu_custom_call" | custom-call | bytes 12582912 | tf_op jit(solution)/shard_map/spectra_rows/pallas_call | solution.py:306
  82.4 12.6 %all-to-all-done.1 = f32[64,3,2,128]{3,2,1,0:T(2,128)S(1)} async-done(((f32[64,3,2,128]{3,2,1,0:T(2,128)}), f32[64,3,2,128]{3,2,1,0:T(2,128)S(1)}, u32[]{:S(2)}, u32[]{:S(2)}) %all-to-all-start.1) | async-done | bytes 196640 | tf_op jit(solution)/shard_map/all_to_all | solution.py:330
  95.0 0.1 reduce_sum.18
  95.1 4.3 %all-gather = f32[6,2,128]{2,1,0:T(2,128)S(1)} all-gather(f32[3,2,128]{2,1,0:T(2,128)S(1)} %reduce_sum.18), channel_id=2, replica_groups=mesh['grp'=4,'z'=8,'xl'=2,'y'=8] {'xl'}, dimensions={0}, use_global_device_ids=true | all-gather | bytes 9216 | tf_op jit(solution)/shard_map/all_gather | solution.py:331
  99.4 0.6 copy.9
  (1 shorter events, 0.0 us)
Async XLA Ops:
  12.6 59.5 %copy-start = (f32[3,512,128]{2,1,0:T(8,128)S(1)}, f32[3,512,128]{2,1,0:T(8,128)}, u32[]{:S(2)}) copy-start(f32[3,512,128]{2,1,0:T(8,128)} %constant.7.clone.turns_ref) | copy-start | bytes 2359300
  12.6 59.5 %copy-start.1 = (bf16[2,256,768]{2,1,0:T(8,128)(2,1)S(1)}, bf16[2,256,768]{2,1,0:T(8,128)(2,1)}, u32[]{:S(2)}) copy-start(bf16[2,256,768]{2,1,0:T(8,128)(2,1)} %constant.6.clone.bases_ref) | copy-start | bytes 2359300
  12.6 59.5 %copy-start.2 = (s32[3]{0:T(128)S(1)}, s32[3]{0:T(128)}, u32[]{:S(2)}) copy-start(s32[3]{0:T(128)} %starts_ref.1) | copy-start | bytes 40
  75.3 19.7 %all-to-all-start.1 = ((f32[64,3,2,128]{3,2,1,0:T(2,128)}), f32[64,3,2,128]{3,2,1,0:T(2,128)S(1)}, u32[]{:S(2)}, u32[]{:S(2)}) async-start(f32[64,3,2,128]{3,2,1,0:T(2,128)} %bitcast.3), calls=%async_computation.1 | async-start | bytes 393216 | tf_op jit(solution)/shard_map/all_to_all | solution.py:330

commit v5 on v3

--- a/solution.py
+++ b/solution.py
@@ -46,17 +46,17 @@
     apart = LANES // QUARTERS
     pieces = x_sems.shape[0]
     width = quarter // pieces
-    chunks = out_sems.shape[0]
+    chunks = out_sems.shape[0] // 2
     size = blocks // chunks
     together = even.shape[0]
 
-    picks_copy = pltpu.make_async_copy(picks_ref, picks, sems.at[0])
-    picks_copy.start()
     x_copies = []
     for piece in range(pieces):
         span = pl.ds(piece * width * QUARTERS, width * QUARTERS)
         x_copies.append(pltpu.make_async_copy(x_ref.at[:, span], x.at[:, span], x_sems.at[piece]))
         x_copies[piece].start()
+    picks_copy = pltpu.make_async_copy(picks_ref, picks, sems.at[0])
+    picks_copy.start()
     picks_copy.wait()
     source = picks[...] // LANES
     index[...] = source // QUARTERS * LANES + picks[...] % LANES
@@ -112,9 +112,9 @@
             before = picked
         return before
 
-    def chunk_copy(chunk):
-        span = pl.ds(chunk * size, size)
-        return pltpu.make_async_copy(out.at[span], out_ref.at[span], out_sems.at[chunk])
+    def batch_copy(i):
+        span = pl.ds(i * together, together)
+        return pltpu.make_async_copy(out.at[span], out_ref.at[span], out_sems.at[i])
 
     def chunk_step(chunk, before):
         for slot, held in enumerate((even, odd)):
@@ -130,19 +130,22 @@
 
                 @pl.when(chunk > 0)
                 def _():
-                    chunk_copy(chunk - 1).start()
+                    batch_copy(2 * chunk - 1).start()
+
+            else:
+                batch_copy(2 * chunk).start()
 
         return before
 
     last = lax.fori_loop(0, chunks, chunk_step, jnp.zeros((LANES, LANES), jnp.float32))
     keep(blocks - 1, last.T)
-    chunk_copy(chunks - 1).start()
-
-    def finish(chunk, carry):
-        chunk_copy(chunk).wait()
+    batch_copy(2 * chunks - 1).start()
+
+    def finish(i, carry):
+        batch_copy(i).wait()
         return carry
 
-    lax.fori_loop(0, chunks, finish, 0)
+    lax.fori_loop(0, 2 * chunks, finish, 0)
 
 
 def gather_points(picks, x):
@@ -167,7 +170,7 @@
             pltpu.SemaphoreType.DMA((1,)),
             pltpu.SemaphoreType.DMA((2,)),
             pltpu.SemaphoreType.DMA((pieces,)),
-            pltpu.SemaphoreType.DMA((4,)),
+            pltpu.SemaphoreType.DMA((8,)),
         ],
         compiler_params=pltpu.CompilerParams(vmem_limit_bytes=58 * 2**20),
         name="gather_points",

time: 100 us -> 100 us (level)
  no operation moved by 1% of the time
where the time goes in v5:
time: 100 us
  blocking collectives  63.8 us (64%)
  Pallas kernels  16.6 us (17%)
  waiting for transfers between devices  12.6 us (13%)
  starting transfers between devices  5.76 us (6%)
    all_to_all x1, blocking collectives, on_device(): arrived = lax.all_to_all(chosen, DEV, 0, 0, tiled=True)  59.5 us
    all_to_all x1, waiting for transfers between devices, on_device(): total = jnp.sum(lax.all_to_all(copies, plane, 0, 0, tiled=True), axis=0)  12.6 us
    pallas_call x1, Pallas kernels, gather_points(): pl.pallas_call(gather_kernel, out_shape=jax.ShapeDtypeStruct((blocks, row...  12.1 us
    all_to_all x1, starting transfers between devices, on_device(): total = jnp.sum(lax.all_to_all(copies, plane, 0, 0, tiled=True), axis=0)  5.76 us
    all_gather x1, blocking collectives, on_device(): total = jnp.sum(lax.all_gather(total, 'xl'), axis=0)  4.33 us
    pallas_call x1, Pallas kernels, window_transforms(): pl.pallas_call(functools.partial(transforms_kernel, points), out_shape=(j...  3.24 us
  transfers between devices with their start and end apart: 1, of which 1 were waited for; matrix products, arithmetic and copies ran while one was open for 0% of the time, Pallas kernels for 1%

profile of v5, /device:TPU:6, one launch (start us, length us, event | category | flops | bytes accessed | tf_op | source)
XLA Modules:
  0.0 100.2 jit_solution(14860975696002728062)
XLA Ops:
  0.6 12.1 %gather_points.1 = f32[128,24,128]{2,1,0:T(8,128)} custom-call(s32[128,128]{1,0:T(8,128)} %bitcast.11, f32[24,16384]{1,0:T(8,128)} %bitcast.10), custom_call_target="tpu_custom_call" | custom-call | tf_op jit(solution)/shard_map/gather_points/pallas_call | solution.py:156
  12.7 0.0 copy-start
  12.7 0.0 copy-start.1
  12.7 0.0 copy-start.2
  12.7 59.5 %all_to_all.10.x_ref = f32[128,24,128]{2,1,0:T(8,128)S(1)} all-to-all(f32[128,24,128]{2,1,0:T(8,128)} %gather_points.1), channel_id=1, replica_groups=mesh['grp'=4,'z'=8,'xl'=2,'y'=8] {'z','xl','y'}, dimensions={0} | all-to-all | bytes 3145728 | tf_op jit(solution)/shard_map/all_to_all | solution.py:329
  72.2 0.0 copy-done
  72.2 0.0 copy-done.1
  72.2 0.0 copy-done.2
  72.2 3.2 %window_transforms.1 = (f32[3,2,256,384]{3,2,1,0:T(8,128)S(1)}, f32[384,128]{1,0:T(8,128)}) custom-call(s32[3]{0:T(128)S(1)} %copy-done.2, f32[128,24,128]{2,1,0:T(8,128)S(1)} %all_to_all.10.x_ref, bf16[2,256,768]{2,1,0:T(8,128)(2,1)S(1)} %copy-done.1, f32[3,512,128]{2,1,0:T(8,128)S(1)} %copy-done), custom_call_target="tpu_custom_call" | custom-call | tf_op jit(solution)/shard_map/window_transforms/pallas_call | solution.py:295
  75.5 5.8 %all-to-all-start.1 = ((f32[64,3,2,128]{3,2,1,0:T(2,128)}), f32[64,3,2,128]{3,2,1,0:T(2,128)S(1)}, u32[]{:S(2)}, u32[]{:S(2)}) async-start(f32[64,3,2,128]{3,2,1,0:T(2,128)} %bitcast.3), calls=%async_computation.1 | async-start | bytes 393216 | tf_op jit(solution)/shard_map/all_to_all | solution.py:334
  81.2 1.3 %spectra_rows.1 = f32[9,256,128]{2,1,0:T(8,128)} custom-call(f32[3,2,256,384]{3,2,1,0:T(8,128)S(1)} %get-tuple-element.4.res_ref), custom_call_target="tpu_custom_call" | custom-call | bytes 12582912 | tf_op jit(solution)/shard_map/spectra_rows/pallas_call | solution.py:310
  82.6 12.6 %all-to-all-done.1 = f32[64,3,2,128]{3,2,1,0:T(2,128)S(1)} async-done(((f32[64,3,2,128]{3,2,1,0:T(2,128)}), f32[64,3,2,128]{3,2,1,0:T(2,128)S(1)}, u32[]{:S(2)}, u32[]{:S(2)}) %all-to-all-start.1) | async-done | bytes 196640 | tf_op jit(solution)/shard_map/all_to_all | solution.py:334
  95.2 0.1 reduce_sum.18
  95.2 4.3 %all-gather = f32[6,2,128]{2,1,0:T(2,128)S(1)} all-gather(f32[3,2,128]{2,1,0:T(2,128)S(1)} %reduce_sum.18), channel_id=2, replica_groups=mesh['grp'=4,'z'=8,'xl'=2,'y'=8] {'xl'}, dimensions={0}, use_global_device_ids=true | all-gather | bytes 9216 | tf_op jit(solution)/shard_map/all_gather | solution.py:335
  99.6 0.6 copy.9
  (1 shorter events, 0.0 us)
Async XLA Ops:
  12.7 59.5 %copy-start = (f32[3,512,128]{2,1,0:T(8,128)S(1)}, f32[3,512,128]{2,1,0:T(8,128)}, u32[]{:S(2)}) copy-start(f32[3,512,128]{2,1,0:T(8,128)} %constant.7.clone.turns_ref) | copy-start | bytes 2359300
  12.7 59.5 %copy-start.1 = (bf16[2,256,768]{2,1,0:T(8,128)(2,1)S(1)}, bf16[2,256,768]{2,1,0:T(8,128)(2,1)}, u32[]{:S(2)}) copy-start(bf16[2,256,768]{2,1,0:T(8,128)(2,1)} %constant.6.clone.bases_ref) | copy-start | bytes 2359300
  12.7 59.5 %copy-start.2 = (s32[3]{0:T(128)S(1)}, s32[3]{0:T(128)}, u32[]{:S(2)}) copy-start(s32[3]{0:T(128)} %starts_ref.1) | copy-start | bytes 40
  75.5 19.7 %all-to-all-start.1 = ((f32[64,3,2,128]{3,2,1,0:T(2,128)}), f32[64,3,2,128]{3,2,1,0:T(2,128)S(1)}, u32[]{:S(2)}, u32[]{:S(2)}) async-start(f32[64,3,2,128]{3,2,1,0:T(2,128)} %bitcast.3), calls=%async_computation.1 | async-start | bytes 393216 | tf_op jit(solution)/shard_map/all_to_all | solution.py:334
